TPU v7x, 32 devices: a whole 2x2x4 slice. The times are simulated.
32 devices in a mesh: dp: 4 (over z), ctx: 8 (over y, x, core).
Axes of the slice: x: 2, y: 2, z: 4, core: 2. Of those that a mesh axis runs over, the one named last changes fastest.
Arguments:
- hidden_in: bfloat16 [4, 1024, 768], P('dp', 'ctx'), may hold values from -6 to 6
- segment_ids: int32 [4, 1024], P('dp', 'ctx'), may hold values from 0 to 4, as said below
- w_qkv: bfloat16 [768, 2304], P('dp'), may hold values from -0.21875 to 0.21875
- w_out: bfloat16 [768, 768], P('dp'), may hold values from -4 to 4
- w_in: bfloat16 [768, 2304], P('dp'), may hold values from -0.21875 to 0.21875
- w_down: bfloat16 [1152, 768], P('dp'), may hold values from -0.1875 to 0.1875
- gain_attn: bfloat16 [768], P('dp'), may hold values from 0.5 to 1.5
- gain_mlp: bfloat16 [768], P('dp'), may hold values from 0.5 to 1.5
- cotangent: bfloat16 [4, 1024, 768], P('dp', 'ctx'), may hold values from -6 to 6
Outputs:
- output: bfloat16 [4, 1024, 768], P('dp', 'ctx')
- grad_input: float32 [4, 1024, 768], P('dp', 'ctx')
- grad_qkv: float32 [768, 2304], P('dp')
- grad_out: float32 [768, 768], P('dp')
- grad_in: float32 [768, 2304], P('dp')
- grad_down: float32 [1152, 768], P('dp')
- grad_gain_attn: float32 [768], P('dp')
- grad_gain_mlp: float32 [768], P('dp')
Inputs may be any that keep to these rules, and one draw needn't show every extreme that they name: `segment_ids`: ids never fall along a sequence; each sequence holds documents 0 to 4; document 2 begins within the first 128 tokens and ends within the last 128; every other document is shorter than 128 tokens.
All inputs are finite; a program needn't handle non-finite values.
Results may differ from a plain program's by a relative error of at most 0.024.
Values may be sent and summed in bfloat16 or wider, within the bound.
A program may use at most 256 MiB of HBM per device.

v0:
```python
import jax
import jax.numpy as jnp
from jax import lax
from jax.sharding import PartitionSpec as P

HEADS = 12
EPSILON = 1e-05
ROPE_THETA = 160000.0
NEGATIVE = -1e30


def layer_norm(values, gain_row):
    average = jnp.mean(values, axis=-1, keepdims=True)
    centred = values - average
    spread = jnp.mean(centred * centred, axis=-1, keepdims=True)
    return centred * lax.rsqrt(spread + EPSILON) * gain_row


def rope_tables(first_row, row_count, head_size):
    position = (first_row + jnp.arange(row_count, dtype=jnp.int32)).astype(jnp.float32)
    frequency = ROPE_THETA ** (-jnp.arange(0, head_size, 2, dtype=jnp.float32) / head_size)
    angles = position[:, None] * frequency[None, :]
    angles = jnp.concatenate([angles, angles], axis=-1)
    return (jnp.cos(angles)[:, None, :], jnp.sin(angles)[:, None, :])


def rotary(values, cosines, sines):
    half_size = values.shape[-1] // 2
    turned = jnp.concatenate([-values[..., half_size:], values[..., :half_size]], axis=-1)
    return values * cosines + turned * sines


def rotary_back(grads, cosines, sines):
    half_size = grads.shape[-1] // 2
    shifted = grads * sines
    return grads * cosines + jnp.concatenate(
        [shifted[..., half_size:], -shifted[..., :half_size]], axis=-1
    )


def geglu(gate_in, gate_up):
    return jax.nn.gelu(gate_in, approximate=False) * gate_up


def contract_rows(left_side, right_side):
    return lax.dot_general(
        left_side, right_side, (((0,), (0,)), ((), ())), preferred_element_type=jnp.float32
    )


def contract_cols(left_side, right_side):
    return lax.dot_general(
        left_side, right_side, (((1,), (1,)), ((), ())), preferred_element_type=jnp.float32
    )


def local(hidden_in, segment_ids, w_qkv, w_out, w_in, w_down, gain_attn, gain_mlp, cotangent):
    local_rows = hidden_in.shape[1]
    model_width = hidden_in.shape[2]
    head_count = HEADS
    head_size = model_width // head_count
    score_scale = head_size ** (-0.5)
    head_shape = (local_rows, head_count, head_size)
    shards = (w_qkv, w_out, w_in, w_down, gain_attn, gain_mlp)
    qkv_full, out_full, in_full, down_full, attn_scale, mlp_scale = (
        lax.all_gather(shards[0], "dp", axis=0, tiled=True),
        lax.all_gather(shards[1], "dp", axis=0, tiled=True),
        lax.all_gather(shards[2], "dp", axis=0, tiled=True),
        lax.all_gather(shards[3], "dp", axis=0, tiled=True),
        lax.all_gather(shards[4], "dp", axis=0, tiled=True),
        lax.all_gather(shards[5], "dp", axis=0, tiled=True),
    )
    hidden_units = in_full.shape[1] // 2
    source = hidden_in[0].astype(jnp.float32)
    own_ids = segment_ids[0]
    cosines, sines = rope_tables(lax.axis_index("ctx") * local_rows, local_rows, head_size)
    normed_one = layer_norm(source, attn_scale.astype(jnp.float32)).astype(jnp.bfloat16)
    projected = jnp.dot(normed_one, qkv_full, preferred_element_type=jnp.float32)
    queries = rotary(projected[:, :model_width].reshape(head_shape), cosines, sines).astype(
        jnp.bfloat16
    )
    own_keys = rotary(
        projected[:, model_width : 2 * model_width].reshape(head_shape), cosines, sines
    ).astype(jnp.bfloat16)
    value_flat = projected[:, 2 * model_width :].astype(jnp.bfloat16)
    own_values = value_flat.reshape(head_shape)
    key_flat = own_keys.reshape(local_rows, model_width)
    query_flat = queries.reshape(local_rows, model_width)
    highest = jnp.full((head_count, local_rows), NEGATIVE, jnp.float32)
    block_keys = lax.all_gather(key_flat, "ctx", axis=0, tiled=True)
    block_values = lax.all_gather(value_flat, "ctx", axis=0, tiled=True)
    block_ids = lax.all_gather(own_ids, "ctx", axis=0, tiled=True)
    piece_rows = block_keys.shape[0]
    scores = (
        jnp.einsum(
            "qhe,khe->hqk",
            queries,
            block_keys.reshape(piece_rows, head_count, head_size),
            preferred_element_type=jnp.float32,
        )
        * score_scale
    )
    allowed = (own_ids[:, None] == block_ids[None, :])[None]
    scores = jnp.where(allowed, scores, NEGATIVE)
    raised = jnp.maximum(highest, jnp.max(scores, axis=-1))
    weights = jnp.where(allowed, jnp.exp(scores - raised[..., None]), 0.0)
    row_total = jnp.sum(weights, axis=-1)
    update = jnp.einsum(
        "hqk,khe->qhe",
        weights.astype(jnp.bfloat16),
        block_values.reshape(piece_rows, head_count, head_size),
        preferred_element_type=jnp.float32,
    )
    summed = update
    highest, row_total, summed = (raised, row_total, summed)
    attention = summed / jnp.transpose(row_total)[:, :, None]
    log_total = highest + jnp.log(row_total)
    attended = attention.reshape(local_rows, model_width).astype(jnp.bfloat16)
    middle = source + jnp.dot(attended, out_full, preferred_element_type=jnp.float32)
    normed_two = layer_norm(middle, mlp_scale.astype(jnp.float32)).astype(jnp.bfloat16)
    lifted = jnp.dot(normed_two, in_full, preferred_element_type=jnp.float32)
    gate_in = lifted[:, :hidden_units]
    gate_up = lifted[:, hidden_units:]
    mixed_units = geglu(gate_in, gate_up).astype(jnp.bfloat16)
    result = (middle + jnp.dot(mixed_units, down_full, preferred_element_type=jnp.float32)).astype(
        jnp.bfloat16
    )
    qkv_back, out_back, in_back, down_back, attn_back, mlp_back = (
        lax.all_gather(shards[0], "dp", axis=0, tiled=True),
        lax.all_gather(shards[1], "dp", axis=0, tiled=True),
        lax.all_gather(shards[2], "dp", axis=0, tiled=True),
        lax.all_gather(shards[3], "dp", axis=0, tiled=True),
        lax.all_gather(shards[4], "dp", axis=0, tiled=True),
        lax.all_gather(shards[5], "dp", axis=0, tiled=True),
    )
    upstream = cotangent[0]
    grad_down = contract_rows(mixed_units, upstream)
    grad_mixed = contract_cols(upstream, down_back)
    _, pull_gate = jax.vjp(geglu, gate_in, gate_up)
    grad_gate_in, grad_gate_up = pull_gate(grad_mixed)
    grad_lifted = jnp.concatenate([grad_gate_in, grad_gate_up], axis=1).astype(jnp.bfloat16)
    grad_in = contract_rows(normed_two, grad_lifted)
    grad_normed_two = contract_cols(grad_lifted, in_back)
    _, pull_two = jax.vjp(layer_norm, middle, mlp_back.astype(jnp.float32))
    grad_middle_part, grad_mlp_gain = pull_two(grad_normed_two)
    grad_middle = upstream.astype(jnp.float32) + grad_middle_part
    grad_branch = grad_middle.astype(jnp.bfloat16)
    grad_out = contract_rows(attended, grad_branch)
    grad_attended = contract_cols(grad_branch, out_back).astype(jnp.bfloat16)
    grad_heads = grad_attended.reshape(head_shape)
    products = jnp.transpose(jnp.sum(grad_heads.astype(jnp.float32) * attention, axis=-1))
    all_log, all_products, all_ids = (
        lax.all_gather(log_total, "ctx", axis=1, tiled=True),
        lax.all_gather(products, "ctx", axis=1, tiled=True),
        lax.all_gather(own_ids, "ctx", axis=0, tiled=True),
    )
    block_keys = lax.all_gather(key_flat, "ctx", axis=0, tiled=True)
    block_values = lax.all_gather(value_flat, "ctx", axis=0, tiled=True)
    block_ids = lax.all_gather(own_ids, "ctx", axis=0, tiled=True)
    piece_rows = block_keys.shape[0]
    key_heads = block_keys.reshape(piece_rows, head_count, head_size)
    scores = (
        jnp.einsum("qhe,khe->hqk", queries, key_heads, preferred_element_type=jnp.float32)
        * score_scale
    )
    allowed = (own_ids[:, None] == block_ids[None, :])[None]
    probabilities = jnp.where(allowed, jnp.exp(scores - log_total[..., None]), 0.0)
    grad_probs = jnp.einsum(
        "qhe,khe->hqk",
        grad_heads,
        block_values.reshape(piece_rows, head_count, head_size),
        preferred_element_type=jnp.float32,
    )
    grad_scores = (probabilities * (grad_probs - products[..., None])).astype(jnp.bfloat16)
    grad_queries = score_scale * jnp.einsum(
        "hqk,khe->qhe", grad_scores, key_heads, preferred_element_type=jnp.float32
    )
    block_queries = lax.all_gather(query_flat, "ctx", axis=0, tiled=True)
    block_grads = lax.all_gather(grad_attended, "ctx", axis=0, tiled=True)
    piece_rows = block_queries.shape[0]
    query_heads = block_queries.reshape(piece_rows, head_count, head_size)
    grad_rows = block_grads.reshape(piece_rows, head_count, head_size)
    scores = (
        jnp.einsum("qhe,khe->hqk", query_heads, own_keys, preferred_element_type=jnp.float32)
        * score_scale
    )
    allowed = (all_ids[:, None] == own_ids[None, :])[None]
    probabilities = jnp.where(allowed, jnp.exp(scores - all_log[..., None]), 0.0)
    grad_values = jnp.einsum(
        "hqk,qhe->khe",
        probabilities.astype(jnp.bfloat16),
        grad_rows,
        preferred_element_type=jnp.float32,
    )
    grad_probs = jnp.einsum(
        "qhe,khe->hqk", grad_rows, own_values, preferred_element_type=jnp.float32
    )
    grad_scores = (probabilities * (grad_probs - all_products[..., None])).astype(jnp.bfloat16)
    grad_keys = score_scale * jnp.einsum(
        "hqk,qhe->khe", grad_scores, query_heads, preferred_element_type=jnp.float32
    )
    grad_keys, grad_values = (grad_keys, grad_values)
    grad_projected = jnp.concatenate(
        [
            rotary_back(grad_queries, cosines, sines).reshape(local_rows, model_width),
            rotary_back(grad_keys, cosines, sines).reshape(local_rows, model_width),
            grad_values.reshape(local_rows, model_width),
        ],
        axis=1,
    ).astype(jnp.bfloat16)
    grad_qkv = contract_rows(normed_one, grad_projected)
    grad_normed_one = contract_cols(grad_projected, qkv_back)
    _, pull_one = jax.vjp(layer_norm, source, attn_back.astype(jnp.float32))
    grad_source, grad_attn_gain = pull_one(grad_normed_one)
    grad_input = grad_middle + grad_source
    local_grads = (grad_qkv, grad_out, grad_in, grad_down, grad_attn_gain, grad_mlp_gain)
    shares = (
        lax.psum_scatter(
            local_grads[0].astype(jnp.bfloat16), "dp", scatter_dimension=0, tiled=True
        ).astype(jnp.float32),
        lax.psum_scatter(
            local_grads[1].astype(jnp.bfloat16), "dp", scatter_dimension=0, tiled=True
        ).astype(jnp.float32),
        lax.psum_scatter(
            local_grads[2].astype(jnp.bfloat16), "dp", scatter_dimension=0, tiled=True
        ).astype(jnp.float32),
        lax.psum_scatter(
            local_grads[3].astype(jnp.bfloat16), "dp", scatter_dimension=0, tiled=True
        ).astype(jnp.float32),
        lax.psum_scatter(
            local_grads[4].astype(jnp.bfloat16), "dp", scatter_dimension=0, tiled=True
        ).astype(jnp.float32),
        lax.psum_scatter(
            local_grads[5].astype(jnp.bfloat16), "dp", scatter_dimension=0, tiled=True
        ).astype(jnp.float32),
    )
    shares = (
        lax.psum(shares[0].astype(jnp.bfloat16), "ctx").astype(jnp.float32),
        lax.psum(shares[1].astype(jnp.bfloat16), "ctx").astype(jnp.float32),
        lax.psum(shares[2].astype(jnp.bfloat16), "ctx").astype(jnp.float32),
        lax.psum(shares[3].astype(jnp.bfloat16), "ctx").astype(jnp.float32),
        lax.psum(shares[4].astype(jnp.bfloat16), "ctx").astype(jnp.float32),
        lax.psum(shares[5].astype(jnp.bfloat16), "ctx").astype(jnp.float32),
    )
    return (
        result[None],
        grad_input[None],
        shares[0],
        shares[1],
        shares[2],
        shares[3],
        shares[4],
        shares[5],
    )


def solution(mesh):
    in_specs = (
        P("dp", "ctx", None),
        P("dp", "ctx"),
        P("dp", None),
        P("dp", None),
        P("dp", None),
        P("dp", None),
        P("dp"),
        P("dp"),
        P("dp", "ctx", None),
    )
    out_specs = (
        P("dp", "ctx", None),
        P("dp", "ctx", None),
        P("dp", None),
        P("dp", None),
        P("dp", None),
        P("dp", None),
        P("dp"),
        P("dp"),
    )
    return jax.shard_map(local, mesh=mesh, in_specs=in_specs, out_specs=out_specs, check_vma=False)
```

profile of v0, /device:TPU:0, one launch (start us, length us, event | category | flops | bytes accessed | tf_op | source)
XLA Modules:
  0.0 630.1 jit_solution(16062213591360769307)
XLA Ops:
  8.0 1.3 fusion.87
  9.9 0.8 dynamic-update-slice
  10.8 0.8 dynamic-update-slice.1
  11.6 13.6 %all-reduce.7 = (bf16[768]{0:T(1024)(128)(2,1)S(1)}, bf16[768]{0:T(1024)(128)(2,1)S(1)}) all-reduce(bf16[768]{0:T(1024)(128)(2,1)S(1)} %dynamic-update-slice, bf16[768]{0:T(1024)(128)(2,1)S(1)} %dynamic-update-slice.1), channel_id=1, replica_groups=mesh['dp'=4,'ctx'=8] {'dp'}, use_global_device_ids=true, to_apply=%add | all-reduce | flops 1536 | bytes 6144
  25.3 0.7 broadcast_multiply_fusion.3
  26.3 1.0 convert_reduce_fusion
  27.3 1.1 fusion.46
  28.5 53.9 %all-gather.10.cloned.1.call-done = bf16[768,2304]{1,0:T(8,128)(2,1)} async-done(((bf16[192,2304]{1,0:T(8,128)(2,1)}), bf16[768,2304]{1,0:T(8,128)(2,1)}) %all-gather.10.cloned.1.call-update) | async-done | bytes 3538960 | tf_op jit(solution)/shard_map/all_gather | solution.py:66
  82.3 2.8 fusion.78
  85.8 0.9 copy.53
  86.7 0.9 copy.49
  87.6 2.0 add_convert_fusion.2
  89.6 0.7 slice.89
  92.2 8.7 %all-gather = s32[1,1024]{1,0:T(1,128)S(1)} all-gather(s32[1,128]{1,0:T(1,128)S(1)} %copy-done.44), channel_id=2, replica_groups=mesh['dp'=4,'ctx'=8] {'ctx'}, dimensions={1}, use_global_device_ids=true | all-gather | bytes 4608 | tf_op jit(solution)/shard_map/all_gather | solution.py:92
  101.1 12.9 %all-gather.14.cloned.1.call-done = bf16[1024,768]{1,0:T(8,128)(2,1)} async-done(((bf16[128,768]{1,0:T(8,128)(2,1)}), bf16[1024,768]{1,0:T(8,128)(2,1)}) %all-gather.14.cloned.1.call-update) | async-done | bytes 1572880 | tf_op jit(solution)/shard_map/all_gather | solution.py:90
  114.0 1.7 copy.50
  115.7 1.3 select_reduce_fusion
  117.1 2.7 copy-done
  119.7 2.0 fusion.1
  121.7 19.9 %all-gather.12.cloned.1.call-done = bf16[1024,768]{1,0:T(8,128)(2,1)} async-done(((bf16[128,768]{1,0:T(8,128)(2,1)}), bf16[1024,768]{1,0:T(8,128)(2,1)}) %all-gather.12.cloned.1.call-update) | async-done | bytes 1572880 | tf_op jit(solution)/shard_map/all_gather | solution.py:91
  141.6 2.6 copy.45
  144.2 5.8 fusion.88
  150.0 23.5 %all-gather.16.cloned.1.call-done = bf16[768,768]{1,0:T(8,128)(2,1)} async-done(((bf16[192,768]{1,0:T(8,128)(2,1)}), bf16[768,768]{1,0:T(8,128)(2,1)}) %all-gather.16.cloned.1.call-update) | async-done | bytes 1179664 | tf_op jit(solution)/shard_map/all_gather | solution.py:67
  173.5 1.7 fusion.89
  176.0 68.1 %all-gather.18.cloned.1.call-done = bf16[768,2304]{1,0:T(8,128)(2,1)} async-done(((bf16[192,2304]{1,0:T(8,128)(2,1)}), bf16[768,2304]{1,0:T(8,128)(2,1)}) %all-gather.18.cloned.1.call-update) | async-done | bytes 3538960 | tf_op jit(solution)/shard_map/all_gather | solution.py:68
  244.1 2.7 fusion.81
  246.8 37.7 %all-gather.20.cloned.1.call-done = bf16[1152,768]{1,0:T(8,128)(2,1)} async-done(((bf16[288,768]{1,0:T(8,128)(2,1)}), bf16[1152,768]{1,0:T(8,128)(2,1)}) %all-gather.20.cloned.1.call-update) | async-done | bytes 1769488 | tf_op jit(solution)/shard_map/all_gather | solution.py:69
  284.5 3.3 add_convert_fusion
  287.8 0.9 multiply_convert_fusion.8
  288.7 1.9 multiply_reduce_fusion
  291.0 1.2 convolution_convert_fusion.4
  292.5 2.4 convolution_convert_fusion.3
  295.0 1.9 convolution_convert_fusion.2
  297.0 3.9 convolution_convert_fusion
  301.0 1.6 broadcast_compare_fusion
  302.6 0.8 copy.56
  303.4 1.1 copy.51
  304.5 7.0 %all-gather.22.cloned.1.call-done = bf16[1024,768]{1,0:T(8,128)(2,1)} async-done(((bf16[128,768]{1,0:T(8,128)(2,1)}), bf16[1024,768]{1,0:T(8,128)(2,1)}) %all-gather.22.cloned.1.call-update) | async-done | bytes 1572880 | tf_op jit(solution)/shard_map/all_gather | solution.py:178
  311.5 2.6 copy.54
  314.1 0.7 log_add_fusion
  314.8 10.1 %all_gather.59 = f32[12,1024]{1,0:T(8,128)} all-gather(f32[12,128]{1,0:T(8,128)S(1)} %log_add_fusion), channel_id=1, replica_groups=mesh['dp'=4,'ctx'=8] {'ctx'}, dimensions={1}, use_global_device_ids=true | all-gather | bytes 55296 | tf_op jit(solution)/shard_map/all_gather | solution.py:153
  324.9 1.1 multiply_reduce_fusion.1
  326.0 9.1 %all_gather.61 = f32[12,1024]{1,0:T(8,128)} all-gather(f32[12,128]{1,0:T(8,128)S(1)} %bitcast.131), channel_id=1, replica_groups=mesh['dp'=4,'ctx'=8] {'ctx'}, dimensions={1}, use_global_device_ids=true | all-gather | bytes 55296 | tf_op jit(solution)/shard_map/all_gather | solution.py:154
  335.0 5.2 fusion.54
  340.3 2.7 copy.55
  343.0 9.0 %fusion.17 = f32[128,12,64]{0,2,1:T(8,128)} fusion(bf16[1024,12,64]{0,2,1:T(8,128)(2,1)} %bitcast.105, f32[12,1024,128]{2,1,0:T(8,128)} %fusion.54, f32[12,1024]{1,0:T(8,128)S(1)} %copy-done.30, f32[12,1024]{1,0:T(8,128)S(1)} %copy-done.28, pred[1024,128]{1,0:T(8,128)(4,1)S(1)} %copy-done.26, bf16[1024,12,64]{0,2,1:T(8,128)(2,1)} %bitcast.114, ...), kind=kOutput, calls=%fused_computation.22 | convolution fusion | flops 412090368 | bytes 10256384 | tf_op jit(solution)/shard_map/hqk,qhe->khe/dot_general | solution.py:199
  352.0 7.1 %broadcast_multiply_fusion.1 = (f32[128,12,64]{0,2,1:T(8,128)}, f32[128,12,64]{0,2,1:T(8,128)S(1)}, f32[128,12,64]{0,2,1:T(8,128)}) fusion(f32[128,64]{0,1:T(8,128)} %get-tuple-element.47, f32[128,12,64]{0,2,1:T(8,128)} %fusion.17, bf16[1024,12,64]{0,2,1:T(8,128)(2,1)S(1)} %bitcast.103, f32[12,128,1024]{2,1,0:T(8,128)} %copy-done, ...), kind=kOutput, calls=%fused_computation.102 | convolution fusion | flops 412286976 | bytes 11382784 | tf_op jit(solution)/shard_map/hqk,khe->qhe/dot_general | solution.py:175
  359.1 1.2 fusion.85
  360.3 1.3 fusion.48
  361.6 5.0 fusion.23
  367.3 3.0 convolution_convert_fusion.1
  371.4 39.2 %reduce-scatter.11.cloned.1.call-done = bf16[288,768]{1,0:T(8,128)(2,1)} async-done(((bf16[1152,768]{1,0:T(8,128)(2,1)}), bf16[288,768]{1,0:T(8,128)(2,1)}) %reduce-scatter.11.cloned.1.call-update) | async-done | bytes 442384 | tf_op jit(solution)/shard_map/reduce_scatter | solution.py:227
  410.7 67.9 %reduce-scatter.9.cloned.1.call-done = bf16[192,2304]{1,0:T(8,128)(2,1)} async-done(((bf16[768,2304]{1,0:T(8,128)(2,1)}), bf16[192,2304]{1,0:T(8,128)(2,1)}) %reduce-scatter.9.cloned.1.call-update) | async-done | bytes 884752 | tf_op jit(solution)/shard_map/reduce_scatter | solution.py:224
  478.6 69.0 %reduce-scatter.5.cloned.1.call-done = bf16[192,2304]{1,0:T(8,128)(2,1)} async-done(((bf16[768,2304]{1,0:T(8,128)(2,1)}), bf16[192,2304]{1,0:T(8,128)(2,1)}) %reduce-scatter.5.cloned.1.call-update) | async-done | bytes 884752 | tf_op jit(solution)/shard_map/reduce_scatter | solution.py:218
  547.6 1.1 fusion.26
  548.7 3.5 fusion.47
  552.6 10.7 %all-reduce.6 = (bf16[768]{0:T(1024)(128)(2,1)S(1)}, bf16[768]{0:T(1024)(128)(2,1)S(1)}) all-reduce(bf16[768]{0:T(1024)(128)(2,1)S(1)} %get-tuple-element.10, bf16[768]{0:T(1024)(128)(2,1)S(1)} %copy-done.43), channel_id=7, replica_groups=mesh['dp'=4,'ctx'=8] {'dp'}, use_global_device_ids=true, to_apply=%region_20.21.clone | all-reduce | flops 1536 | bytes 6144
  563.5 12.1 %all-reduce.4 = (bf16[192]{0:T(256)(128)(2,1)S(1)}, bf16[192]{0:T(256)(128)(2,1)S(1)}) all-reduce(bf16[192]{0:T(256)(128)(2,1)S(1)} %dynamic-slice.3, bf16[192]{0:T(256)(128)(2,1)S(1)} %dynamic-slice.5), channel_id=1, replica_groups=mesh['dp'=4,'ctx'=8] {'ctx'}, use_global_device_ids=true, to_apply=%region_21.22 | all-reduce | flops 384 | bytes 1536 | tf_op jit(solution)/shard_map/psum | solution.py:242
  576.7 1.0 add_bitcast_fusion
  577.7 39.2 %all-reduce.10.cloned.1.call-done = (bf16[192,2304]{1,0:T(8,128)(2,1)}, bf16[192,768]{1,0:T(8,128)(2,1)}, bf16[192,2304]{1,0:T(8,128)(2,1)}, bf16[288,768]{1,0:T(8,128)(2,1)}) async-done(((bf16[192,2304]{1,0:T(8,128)(2,1)}, bf16[192,768]{1,0:T(8,128)(2,1)}, bf16[192,2304]{1,0:T(8,128)(2,1)}, bf16[288,768]{1,0:T(8,128)(2,1)}), (bf16[192,2304]{1,0:T(8,128)(2,1)}, bf16[192,768]{1,0:T(8,128)(2,1)}, ...) | async-done | bytes 2506768 | tf_op jit(solution)/shard_map/psum | solution.py:238
  616.9 2.6 convert_element_type.150
  619.5 1.8 convert_element_type.152
  621.3 1.3 convert_element_type.154
  622.6 1.0 convert_element_type.156
  (162 shorter events, 7.9 us)
Async XLA Ops:
  7.2 75.2 %all-gather.10.cloned.1.call-start = ((), (), s32[]{:S(2)}) async-start(), calls=%async_computation.4 | async-start | bytes 4423680 | tf_op jit(solution)/shard_map/all_gather | solution.py:66
  7.9 106.1 %all-gather.14.cloned.1.call-start = ((), (), s32[]{:S(2)}) async-start(), calls=%async_computation.6 | async-start | bytes 1769472 | tf_op jit(solution)/shard_map/all_gather | solution.py:90
  26.1 89.7 %copy-start.22 = (f32[128,64]{0,1:T(8,128)}, f32[128,64]{0,1:T(8,128)S(1)}, u32[]{:S(2)}) copy-start(f32[128,64]{0,1:T(8,128)S(1)} %get-tuple-element.49) | copy-start | bytes 98308
  27.3 57.9 %copy-start.34 = (f32[128]{0:T(128)}, f32[128]{0:T(128)S(1)}, u32[]{:S(2)}) copy-start(f32[128]{0:T(128)S(1)} %broadcast_multiply_fusion.6) | copy-start | bytes 1540
  28.4 56.8 %copy-start.47 = (f32[128]{0:T(128)}, f32[128]{0:T(128)S(1)}, u32[]{:S(2)}) copy-start(f32[128]{0:T(128)S(1)} %fusion.46) | copy-start | bytes 1540
  28.5 56.8 %copy-start.36 = (f32[128]{0:T(128)}, f32[128]{0:T(128)S(1)}, u32[]{:S(2)}) copy-start(f32[128]{0:T(128)S(1)} %fusion.62) | copy-start | bytes 1540
  85.4 4.1 copy-start.4
  85.7 6.4 %copy-start.6 = (f32[128,12,64]{0,2,1:T(8,128)}, f32[128,12,64]{0,2,1:T(8,128)S(1)}, u32[]{:S(2)}) copy-start(f32[128,12,64]{0,2,1:T(8,128)S(1)} %get-tuple-element.45) | copy-start | bytes 1179652
  85.7 6.4 %copy-start.44 = (s32[1,128]{1,0:T(1,128)S(1)}, s32[1,128]{1,0:T(1,128)}, u32[]{:S(2)}) copy-start(s32[1,128]{1,0:T(1,128)} %param.10) | copy-start | bytes 1540
  89.6 52.1 %all-gather.12.cloned.1.call-start = ((), (), s32[]{:S(2)}) async-start(), calls=%async_computation.5 | async-start | bytes 1769472 | tf_op jit(solution)/shard_map/all_gather | solution.py:91
  90.4 83.2 %all-gather.16.cloned.1.call-start = ((), (), s32[]{:S(2)}) async-start(), calls=%async_computation.7 | async-start | bytes 1474560 | tf_op jit(solution)/shard_map/all_gather | solution.py:67
  90.9 153.2 %all-gather.18.cloned.1.call-start = ((), (), s32[]{:S(2)}) async-start(), calls=%async_computation.8 | async-start | bytes 4423680 | tf_op jit(solution)/shard_map/all_gather | solution.py:68
  91.5 192.9 %all-gather.20.cloned.1.call-start = ((), (), s32[]{:S(2)}) async-start(), calls=%async_computation.9 | async-start | bytes 2211840 | tf_op jit(solution)/shard_map/all_gather | solution.py:69
  92.1 219.4 %all-gather.22.cloned.1.call-start = ((), (), s32[]{:S(2)}) async-start(), calls=%async_computation.10 | async-start | bytes 1769472 | tf_op jit(solution)/shard_map/all_gather | solution.py:178
  100.9 16.1 %copy-start.31 = (s32[1,1024]{1,0:T(1,128)}, s32[1,1024]{1,0:T(1,128)S(1)}, u32[]{:S(2)}) copy-start(s32[1,1024]{1,0:T(1,128)S(1)} %all-gather) | copy-start | bytes 12292
  101.0 43.2 %copy-start.17 = (pred[128,1024]{1,0:T(8,128)(4,1)}, pred[128,1024]{1,0:T(8,128)(4,1)S(1)}, u32[]{:S(2)}) copy-start(pred[128,1024]{1,0:T(8,128)(4,1)S(1)} %broadcast_compare_fusion.1) | copy-start | bytes 393220
  101.1 239.2 %all-gather.24.cloned.1.call-start = ((), (), s32[]{:S(2)}) async-start(), calls=%async_computation.11 | async-start | bytes 1769472 | tf_op jit(solution)/shard_map/all_gather | solution.py:179
  117.0 2.7 copy-start
  121.7 28.3 %copy-start.32 = (f32[12,128]{1,0:T(8,128)}, f32[12,128]{1,0:T(8,128)S(1)}, u32[]{:S(2)}) copy-start(f32[12,128]{1,0:T(8,128)S(1)} %fusion.1) | copy-start | bytes 18436
  144.2 29.3 %copy-start.2 = (bf16[1,128,768]{2,1,0:T(8,128)(2,1)S(1)}, bf16[1,128,768]{2,1,0:T(8,128)(2,1)}, u32[]{:S(2)}) copy-start(bf16[1,128,768]{2,1,0:T(8,128)(2,1)} %param.9) | copy-start | bytes 589828
  150.0 26.0 %copy-start.21 = (bf16[128,12,64]{0,2,1:T(8,128)(2,1)}, bf16[128,12,64]{0,2,1:T(8,128)(2,1)S(1)}, u32[]{:S(2)}) copy-start(bf16[128,12,64]{0,2,1:T(8,128)(2,1)S(1)} %get-tuple-element.54) | copy-start | bytes 589828
  175.2 109.2 %copy-start.14 = (bf16[1,128,768]{2,1,0:T(8,128)(2,1)S(1)}, bf16[1,128,768]{2,1,0:T(8,128)(2,1)}, u32[]{:S(2)}) copy-start(bf16[1,128,768]{2,1,0:T(8,128)(2,1)} %param.17) | copy-start | bytes 589828
  175.3 0.7 copy-start.38
  175.5 0.5 copy-start.49
  284.5 4.2 copy-start.1
  284.5 4.2 copy-start.39
  284.5 4.2 copy-start.41
  287.8 2.8 copy-start.19
  288.7 2.3 copy-start.8
  288.7 1.9 copy-start.50
  288.7 2.3 copy-start.3
  290.6 4.4 copy-start.10
  290.8 1.4 copy-start.45
  292.3 4.7 copy-start.9
  292.3 79.2 %reduce-scatter.7.cloned.1.call-start = ((), (), s32[]{:S(2)}) async-start(), calls=%async_computation.13 | async-start | bytes 1474560 | tf_op jit(solution)/shard_map/reduce_scatter | solution.py:221
  294.9 2.0 copy-start.40
  294.9 2.1 copy-start.42
  294.9 115.8 %reduce-scatter.11.cloned.1.call-start = ((), (), s32[]{:S(2)}) async-start(), calls=%async_computation.15 | async-start | bytes 2211840 | tf_op jit(solution)/shard_map/reduce_scatter | solution.py:227
  296.9 5.7 copy-start.12
  296.9 181.7 %reduce-scatter.9.cloned.1.call-start = ((), (), s32[]{:S(2)}) async-start(), calls=%async_computation.14 | async-start | bytes 4423680 | tf_op jit(solution)/shard_map/reduce_scatter | solution.py:224
  300.9 34.1 %copy-start.5 = (f32[128,768]{0,1:T(8,128)S(1)}, f32[128,768]{0,1:T(8,128)}, u32[]{:S(2)}) copy-start(f32[128,768]{0,1:T(8,128)} %copy-done.4) | copy-start | bytes 1179652
  300.9 34.1 %copy-start.7 = (f32[128,12,64]{0,2,1:T(8,128)S(1)}, f32[128,12,64]{0,2,1:T(8,128)}, u32[]{:S(2)}) copy-start(f32[128,12,64]{0,2,1:T(8,128)} %copy-done.6) | copy-start | bytes 1179652
  300.9 246.6 %reduce-scatter.5.cloned.1.call-start = ((), (), s32[]{:S(2)}) async-start(), calls=%async_computation.12 | async-start | bytes 4423680 | tf_op jit(solution)/shard_map/reduce_scatter | solution.py:218
  314.8 10.1 %copy-start.33 = (f32[12,128]{1,0:T(8,128)}, f32[12,128]{1,0:T(8,128)S(1)}, u32[]{:S(2)}) copy-start(f32[12,128]{1,0:T(8,128)S(1)} %log_add_fusion) | copy-start | bytes 18436
  340.2 2.7 copy-start.25
  340.2 2.7 copy-start.26
  340.2 2.7 copy-start.28
  340.2 2.7 copy-start.30
  343.0 9.0 %copy-start.18 = (pred[128,1024]{1,0:T(8,128)(4,1)S(1)}, pred[128,1024]{1,0:T(8,128)(4,1)}, u32[]{:S(2)}) copy-start(pred[128,1024]{1,0:T(8,128)(4,1)} %copy-done.17) | copy-start | bytes 393220
  359.1 2.5 copy-start.16
  359.1 2.5 copy-start.27
  359.1 2.5 copy-start.29
  361.6 5.7 copy-start.35
  361.6 5.7 copy-start.37
  366.6 0.7 copy-start.24
  370.3 177.3 %copy-start.11 = (bf16[128,1152]{1,0:T(8,128)(2,1)S(1)}, bf16[128,1152]{1,0:T(8,128)(2,1)}, u32[]{:S(2)}) copy-start(bf16[128,1152]{1,0:T(8,128)(2,1)} %get-tuple-element.27) | copy-start | bytes 884740
  370.3 177.3 %copy-start.13 = (bf16[1152,768]{1,0:T(8,128)(2,1)S(1)}, bf16[1152,768]{1,0:T(8,128)(2,1)}, u32[]{:S(2)}) copy-start(bf16[1152,768]{1,0:T(8,128)(2,1)} %all-gather.20.cloned.1.call-done) | copy-start | bytes 5308420
  370.3 246.5 %all-reduce.10.cloned.1.call-start = ((), (), s32[]{:S(2)}) async-start(), calls=%async_computation.16 | async-start | bytes 5013504 | tf_op jit(solution)/shard_map/psum | solution.py:238
  548.7 3.5 copy-start.48
  548.7 3.8 copy-start.43
  548.7 28.0 %copy-start.15 = (bf16[1,128,768]{2,1,0:T(8,128)(2,1)S(1)}, bf16[1,128,768]{2,1,0:T(8,128)(2,1)}, u32[]{:S(2)}) copy-start(bf16[1,128,768]{2,1,0:T(8,128)(2,1)} %param.17) | copy-start | bytes 589828
  548.7 28.0 %copy-start.46 = (f32[128]{0:T(128)S(1)}, f32[128]{0:T(128)}, u32[]{:S(2)}) copy-start(f32[128]{0:T(128)} %copy-done.45) | copy-start | bytes 1540
  616.9 4.4 copy-start.20
  616.9 5.7 copy-start.23
Sparse Core Ops, SparseCore 0:
  9.6 72.7 all-gather.9
  89.7 24.2 all-gather.13
  115.9 25.6 all-gather.11
  143.0 30.4 all-gather.15
  174.9 69.0 all-gather.17
  245.5 38.8 all-gather.19
  286.9 24.5 all-gather.21
  313.4 25.8 all-gather.23
  341.6 29.1 reduce-scatter.6
  373.6 37.0 reduce-scatter.10
  413.1 65.4 reduce-scatter.8
  480.9 66.6 reduce-scatter.4
  551.7 65.0 all-reduce.9
where the time goes:
time: 631 us; the launch traced here: 630 us
  waiting for transfers between devices  441 us (70%)
  blocking collectives  64.3 us (10%)
  matrix products  62.8 us (10%)
  other arithmetic  24.1 us (4%)
  local copies, waits for them, and re-layouts  21.3 us (3%)
  between operations  16 us (3%)
    reduce_scatter x1, waiting for transfers between devices, local(): lax.psum_scatter(local_grads[0].astype(jnp.bfloat16), 'dp', scatter_dimen...  69 us
    all_gather x1, waiting for transfers between devices, local(): lax.all_gather(shards[2], 'dp', axis=0, tiled=True)  68.1 us
    reduce_scatter x1, waiting for transfers between devices, local(): lax.psum_scatter(local_grads[2].astype(jnp.bfloat16), 'dp', scatter_dimen...  67.9 us
    all_gather x1, waiting for transfers between devices, local(): lax.all_gather(shards[0], 'dp', axis=0, tiled=True)  53.9 us
    reduce_scatter x1, waiting for transfers between devices, local(): lax.psum_scatter(local_grads[3].astype(jnp.bfloat16), 'dp', scatter_dimen...  39.2 us
    psum x1, waiting for transfers between devices, local(): lax.psum(shares[0].astype(jnp.bfloat16), 'ctx').astype(jnp.float32)  39.2 us
    all_gather x1, waiting for transfers between devices, local(): lax.all_gather(shards[3], 'dp', axis=0, tiled=True)  37.7 us
    unnamed x2, blocking collectives  24.3 us
  transfers between devices with their start and end apart: 13, of which 11 were waited for; matrix products, arithmetic and copies ran while one was open for 14% of the time, Pallas kernels for 0%

commit v1 on v0

--- a/solution.py
+++ b/solution.py
@@ -62,10 +62,25 @@
     score_scale = head_size ** (-0.5)
     head_shape = (local_rows, head_count, head_size)
     shards = (w_qkv, w_out, w_in, w_down, gain_attn, gain_mlp)
+
+    def enter_the_area(load):
+        mesh_dim = "dp"
+        p_next, y_new = (lax.axis_size(mesh_dim), lax.axis_index(mesh_dim))
+        later, current_arr = (load, 1)
+        while current_arr < p_next:
+            wide_out = lax.ppermute(
+                later, mesh_dim, [(jj, jj ^ current_arr) for jj in range(p_next)]
+            )
+            all_rows = jnp.concatenate([later, wide_out], 0)
+            next_value = jnp.concatenate([wide_out, later], 0)
+            later = jnp.where(y_new & current_arr == 0, all_rows, next_value)
+            current_arr = 2 * current_arr
+        return later
+
     qkv_full, out_full, in_full, down_full, attn_scale, mlp_scale = (
         lax.all_gather(shards[0], "dp", axis=0, tiled=True),
         lax.all_gather(shards[1], "dp", axis=0, tiled=True),
-        lax.all_gather(shards[2], "dp", axis=0, tiled=True),
+        enter_the_area(shards[2]),
         lax.all_gather(shards[3], "dp", axis=0, tiled=True),
         lax.all_gather(shards[4], "dp", axis=0, tiled=True),
         lax.all_gather(shards[5], "dp", axis=0, tiled=True),

time: 631 us -> 658 us (1.043)
  waiting for transfers between devices: 441 us -> 456 us
  matrix products: 62.8 us -> 70.7 us
    ppermute x0 -> x2, waiting for transfers between devices: none -> 67.3 us  [enter_the_area(): lax.ppermute(later, mesh_dim, [(jj, jj ^ current_arr) for jj in range(p_n...]
    all_gather x1, waiting for transfers between devices: 37.7 us -> 0.02 us  [local(): lax.all_gather(shards[3], 'dp', axis=0, tiled=True)]
    all_gather x1, waiting for transfers between devices: 23.5 us -> 36.7 us  [local(): lax.all_gather(shards[1], 'dp', axis=0, tiled=True)]
    all_gather x1, waiting for transfers between devices: 12.9 us -> 0.02 us  [local(): block_keys = lax.all_gather(key_flat, 'ctx', axis=0, tiled=True)]
    all_gather x1, waiting for transfers between devices: 68.1 us -> 59.4 us  [local(): lax.all_gather(shards[2], 'dp', axis=0, tiled=True)]
  transfers between devices with their start and end apart: 13 -> 15, of which waited for: 11 -> 11; matrix products, arithmetic and copies ran while one was open for 14% -> 15% of each run, Pallas kernels for 0% -> 0%
where the time goes in v1:
time: 658 us
  waiting for transfers between devices  456 us (69%)
  matrix products  70.7 us (11%)
  blocking collectives  64.6 us (10%)
  other arithmetic  26.6 us (4%)
  local copies, waits for them, and re-layouts  21.6 us (3%)
  between operations  15.9 us (2%)
    reduce_scatter x1, waiting for transfers between devices, local(): lax.psum_scatter(local_grads[0].astype(jnp.bfloat16), 'dp', scatter_dimen...  69 us
    reduce_scatter x1, waiting for transfers between devices, local(): lax.psum_scatter(local_grads[2].astype(jnp.bfloat16), 'dp', scatter_dimen...  67.9 us
    ppermute x2, waiting for transfers between devices, enter_the_area(): lax.ppermute(later, mesh_dim, [(jj, jj ^ current_arr) for jj in range(p_n...  67.3 us
    all_gather x1, waiting for transfers between devices, local(): lax.all_gather(shards[2], 'dp', axis=0, tiled=True)  59.4 us
    all_gather x1, waiting for transfers between devices, local(): lax.all_gather(shards[0], 'dp', axis=0, tiled=True)  53.9 us
    reduce_scatter x1, waiting for transfers between devices, local(): lax.psum_scatter(local_grads[3].astype(jnp.bfloat16), 'dp', scatter_dimen...  39.2 us
    psum x1, waiting for transfers between devices, local(): lax.psum(shares[0].astype(jnp.bfloat16), 'ctx').astype(jnp.float32)  37.9 us
    all_gather x1, waiting for transfers between devices, local(): lax.all_gather(shards[1], 'dp', axis=0, tiled=True)  36.7 us
  transfers between devices with their start and end apart: 15, of which 11 were waited for; matrix products, arithmetic and copies ran while one was open for 15% of the time, Pallas kernels for 0%

profile of v1, /device:TPU:0, one launch (start us, length us, event | category | flops | bytes accessed | tf_op | source)
XLA Modules:
  0.0 657.5 jit_solution(431908387409664196)
XLA Ops:
  8.0 1.3 fusion.94
  9.9 0.8 dynamic-update-slice
  10.8 0.8 dynamic-update-slice.1
  11.6 13.6 %all-reduce.7 = (bf16[768]{0:T(1024)(128)(2,1)S(1)}, bf16[768]{0:T(1024)(128)(2,1)S(1)}) all-reduce(bf16[768]{0:T(1024)(128)(2,1)S(1)} %dynamic-update-slice, bf16[768]{0:T(1024)(128)(2,1)S(1)} %dynamic-update-slice.1), channel_id=1, replica_groups=mesh['dp'=4,'ctx'=8] {'dp'}, use_global_device_ids=true, to_apply=%add | all-reduce | flops 1536 | bytes 6144
  25.3 0.7 broadcast_multiply_fusion.3
  26.3 1.0 convert_reduce_fusion
  27.3 1.1 fusion.53
  28.5 53.9 %all-gather.10.cloned.1.call-done = bf16[768,2304]{1,0:T(8,128)(2,1)} async-done(((bf16[192,2304]{1,0:T(8,128)(2,1)}), bf16[768,2304]{1,0:T(8,128)(2,1)}) %all-gather.10.cloned.1.call-update) | async-done | bytes 3538960 | tf_op jit(solution)/shard_map/all_gather | solution.py:81
  82.4 2.8 fusion.86
  85.9 0.9 copy.49
  86.8 1.8 add_convert_fusion.2
  91.4 8.7 %all-gather = s32[1,1024]{1,0:T(1,128)S(1)} all-gather(s32[1,128]{1,0:T(1,128)S(1)} %copy-done.42), channel_id=2, replica_groups=mesh['dp'=4,'ctx'=8] {'ctx'}, dimensions={1}, use_global_device_ids=true | all-gather | bytes 4608 | tf_op jit(solution)/shard_map/all_gather | solution.py:107
  100.3 12.6 %collective-permute-done = bf16[192,2304]{1,0:T(8,128)(2,1)S(1)} collective-permute-done((bf16[192,2304]{1,0:T(8,128)(2,1)}, bf16[192,2304]{1,0:T(8,128)(2,1)S(1)}, u32[]{:S(2)}, u32[]{:S(2)}) %collective-permute-start) | collective-permute-done | bytes 884768 | tf_op jit(solution)/shard_map/ppermute | solution.py:71
  112.9 3.3 maximum_select_fusion.2
  116.2 1.1 collective-permute-start.1
  117.5 1.7 copy.50
  119.3 1.3 select_reduce_fusion
  120.6 2.7 copy-done
  123.3 2.0 fusion.1
  125.2 15.5 %all-gather.12.cloned.1.call-done = bf16[1024,768]{1,0:T(8,128)(2,1)} async-done(((bf16[128,768]{1,0:T(8,128)(2,1)}), bf16[1024,768]{1,0:T(8,128)(2,1)}) %all-gather.12.cloned.1.call-update) | async-done | bytes 1572880 | tf_op jit(solution)/shard_map/all_gather | solution.py:106
  140.8 2.6 copy.45
  143.3 5.8 fusion.95
  149.1 36.7 %all-gather.16.cloned.1.call-done = bf16[768,768]{1,0:T(8,128)(2,1)} async-done(((bf16[192,768]{1,0:T(8,128)(2,1)}), bf16[768,768]{1,0:T(8,128)(2,1)}) %all-gather.16.cloned.1.call-update) | async-done | bytes 1179664 | tf_op jit(solution)/shard_map/all_gather | solution.py:82
  185.8 1.7 fusion.96
  187.8 54.7 %collective-permute-done.1 = bf16[384,2304]{1,0:T(8,128)(2,1)} collective-permute-done((bf16[384,2304]{1,0:T(8,128)(2,1)}, bf16[384,2304]{1,0:T(8,128)(2,1)}, u32[]{:S(2)}, u32[]{:S(2)}) %collective-permute-start.1) | collective-permute-done | bytes 1769504 | tf_op jit(solution)/shard_map/ppermute | solution.py:71
  242.5 5.5 fusion.3
  248.1 3.8 add_convert_fusion
  251.9 0.8 multiply_convert_fusion.8
  252.7 59.4 %all-gather.20.cloned.1.call-done = bf16[768,2304]{1,0:T(8,128)(2,1)} async-done(((bf16[192,2304]{1,0:T(8,128)(2,1)}), bf16[768,2304]{1,0:T(8,128)(2,1)}) %all-gather.20.cloned.1.call-update) | async-done | bytes 3538960 | tf_op jit(solution)/shard_map/all_gather | solution.py:146
  312.2 4.1 multiply_reduce_fusion
  317.2 1.2 convolution_convert_fusion.4
  318.5 2.4 convolution_convert_fusion.3
  321.0 2.9 convolution_convert_fusion.2
  323.9 4.1 convolution_convert_fusion
  328.7 1.5 broadcast_compare_fusion
  330.2 0.8 copy.56
  331.0 1.1 copy.51
  332.1 6.8 %all-gather.22.cloned.1.call-done = bf16[1024,768]{1,0:T(8,128)(2,1)} async-done(((bf16[128,768]{1,0:T(8,128)(2,1)}), bf16[1024,768]{1,0:T(8,128)(2,1)}) %all-gather.22.cloned.1.call-update) | async-done | bytes 1572880 | tf_op jit(solution)/shard_map/all_gather | solution.py:193
  338.9 2.6 copy.54
  341.5 0.7 log_add_fusion
  342.2 10.3 %all_gather.58 = f32[12,1024]{1,0:T(8,128)} all-gather(f32[12,128]{1,0:T(8,128)S(1)} %log_add_fusion), channel_id=1, replica_groups=mesh['dp'=4,'ctx'=8] {'ctx'}, dimensions={1}, use_global_device_ids=true | all-gather | bytes 55296 | tf_op jit(solution)/shard_map/all_gather | solution.py:168
  352.5 1.1 multiply_reduce_fusion.1
  353.5 9.3 %all_gather.60 = f32[12,1024]{1,0:T(8,128)} all-gather(f32[12,128]{1,0:T(8,128)S(1)} %bitcast.130), channel_id=1, replica_groups=mesh['dp'=4,'ctx'=8] {'ctx'}, dimensions={1}, use_global_device_ids=true | all-gather | bytes 55296 | tf_op jit(solution)/shard_map/all_gather | solution.py:169
  362.8 5.2 fusion.61
  368.1 2.7 copy.55
  370.8 9.0 %fusion.24 = f32[128,12,64]{0,2,1:T(8,128)} fusion(bf16[1024,12,64]{0,2,1:T(8,128)(2,1)} %bitcast.104, f32[12,1024,128]{2,1,0:T(8,128)} %fusion.61, f32[12,1024]{1,0:T(8,128)S(1)} %copy-done.28, f32[12,1024]{1,0:T(8,128)S(1)} %copy-done.26, pred[1024,128]{1,0:T(8,128)(4,1)S(1)} %copy-done.24, bf16[1024,12,64]{0,2,1:T(8,128)(2,1)} %bitcast.113, ...), kind=kOutput, calls=%fused_computation.31 | convolution fusion | flops 412090368 | bytes 10256384 | tf_op jit(solution)/shard_map/hqk,qhe->khe/dot_general | solution.py:214
  379.7 7.0 %broadcast_multiply_fusion.1 = (f32[128,12,64]{0,2,1:T(8,128)S(1)}, f32[128,12,64]{0,2,1:T(8,128)}, f32[128,12,64]{0,2,1:T(8,128)}) fusion(f32[128,64]{0,1:T(8,128)} %get-tuple-element.47, f32[128,12,64]{0,2,1:T(8,128)} %fusion.24, bf16[1024,12,64]{0,2,1:T(8,128)(2,1)S(1)} %bitcast.102, f32[12,128,1024]{2,1,0:T(8,128)} %copy-done, ...), kind=kOutput, calls=%fused_computation.111 | convolution fusion | flops 412286976 | bytes 11382784 | tf_op jit(solution)/shard_map/hqk,khe->qhe/dot_general | solution.py:190
  386.8 1.2 fusion.93
  388.0 1.3 fusion.55
  389.3 5.0 fusion.30
  395.0 3.0 convolution_convert_fusion.1
  399.0 39.2 %reduce-scatter.11.cloned.1.call-done = bf16[288,768]{1,0:T(8,128)(2,1)} async-done(((bf16[1152,768]{1,0:T(8,128)(2,1)}), bf16[288,768]{1,0:T(8,128)(2,1)}) %reduce-scatter.11.cloned.1.call-update) | async-done | bytes 442384 | tf_op jit(solution)/shard_map/reduce_scatter | solution.py:242
  438.1 67.9 %reduce-scatter.9.cloned.1.call-done = bf16[192,2304]{1,0:T(8,128)(2,1)} async-done(((bf16[768,2304]{1,0:T(8,128)(2,1)}), bf16[192,2304]{1,0:T(8,128)(2,1)}) %reduce-scatter.9.cloned.1.call-update) | async-done | bytes 884752 | tf_op jit(solution)/shard_map/reduce_scatter | solution.py:239
  506.1 69.0 %reduce-scatter.5.cloned.1.call-done = bf16[192,2304]{1,0:T(8,128)(2,1)} async-done(((bf16[768,2304]{1,0:T(8,128)(2,1)}), bf16[192,2304]{1,0:T(8,128)(2,1)}) %reduce-scatter.5.cloned.1.call-update) | async-done | bytes 884752 | tf_op jit(solution)/shard_map/reduce_scatter | solution.py:233
  575.1 2.6 fusion.33
  577.7 3.4 fusion.54
  581.4 10.7 %all-reduce.6 = (bf16[768]{0:T(1024)(128)(2,1)S(1)}, bf16[768]{0:T(1024)(128)(2,1)S(1)}) all-reduce(bf16[768]{0:T(1024)(128)(2,1)S(1)} %get-tuple-element.10, bf16[768]{0:T(1024)(128)(2,1)S(1)} %copy-done.39), channel_id=7, replica_groups=mesh['dp'=4,'ctx'=8] {'dp'}, use_global_device_ids=true, to_apply=%region_20.21.clone | all-reduce | flops 1536 | bytes 6144
  592.3 11.9 %all-reduce.4 = (bf16[192]{0:T(256)(128)(2,1)S(1)}, bf16[192]{0:T(256)(128)(2,1)S(1)}) all-reduce(bf16[192]{0:T(256)(128)(2,1)S(1)} %dynamic-slice.3, bf16[192]{0:T(256)(128)(2,1)S(1)} %dynamic-slice.5), channel_id=1, replica_groups=mesh['dp'=4,'ctx'=8] {'ctx'}, use_global_device_ids=true, to_apply=%region_21.22 | all-reduce | flops 384 | bytes 1536 | tf_op jit(solution)/shard_map/psum | solution.py:257
  605.4 1.0 add_bitcast_fusion
  606.4 37.9 %all-reduce.10.cloned.1.call-done = (bf16[192,2304]{1,0:T(8,128)(2,1)}, bf16[192,768]{1,0:T(8,128)(2,1)}, bf16[192,2304]{1,0:T(8,128)(2,1)}, bf16[288,768]{1,0:T(8,128)(2,1)}) async-done(((bf16[192,2304]{1,0:T(8,128)(2,1)}, bf16[192,768]{1,0:T(8,128)(2,1)}, bf16[192,2304]{1,0:T(8,128)(2,1)}, bf16[288,768]{1,0:T(8,128)(2,1)}), (bf16[192,2304]{1,0:T(8,128)(2,1)}, bf16[192,768]{1,0:T(8,128)(2,1)}, ...) | async-done | bytes 2506768 | tf_op jit(solution)/shard_map/psum | solution.py:253
  644.3 2.6 convert_element_type.150
  646.9 1.8 convert_element_type.152
  648.7 1.3 convert_element_type.154
  650.0 1.0 convert_element_type.156
  (163 shorter events, 9.5 us)
Async XLA Ops:
  7.2 75.2 %all-gather.10.cloned.1.call-start = ((), (), s32[]{:S(2)}) async-start(), calls=%async_computation.4 | async-start | bytes 4423680 | tf_op jit(solution)/shard_map/all_gather | solution.py:81
  7.9 109.6 %all-gather.14.cloned.1.call-start = ((), (), s32[]{:S(2)}) async-start(), calls=%async_computation.6 | async-start | bytes 1769472 | tf_op jit(solution)/shard_map/all_gather | solution.py:105
  26.0 56.3 %copy-start.18 = (f32[128,64]{0,1:T(8,128)}, f32[128,64]{0,1:T(8,128)S(1)}, u32[]{:S(2)}) copy-start(f32[128,64]{0,1:T(8,128)S(1)} %get-tuple-element.49) | copy-start | bytes 98308
  27.3 55.0 %copy-start.33 = (f32[128]{0:T(128)}, f32[128]{0:T(128)S(1)}, u32[]{:S(2)}) copy-start(f32[128]{0:T(128)S(1)} %broadcast_multiply_fusion.6) | copy-start | bytes 1540
  28.4 53.9 %copy-start.45 = (f32[128]{0:T(128)}, f32[128]{0:T(128)S(1)}, u32[]{:S(2)}) copy-start(f32[128]{0:T(128)S(1)} %fusion.53) | copy-start | bytes 1540
  28.5 53.9 %copy-start.35 = (f32[128]{0:T(128)}, f32[128]{0:T(128)S(1)}, u32[]{:S(2)}) copy-start(f32[128]{0:T(128)S(1)} %fusion.69) | copy-start | bytes 1540
  85.7 5.5 copy-start.3
  85.7 5.6 copy-start.42
  88.7 52.1 %all-gather.12.cloned.1.call-start = ((), (), s32[]{:S(2)}) async-start(), calls=%async_computation.5 | async-start | bytes 1769472 | tf_op jit(solution)/shard_map/all_gather | solution.py:106
  89.4 96.4 %all-gather.16.cloned.1.call-start = ((), (), s32[]{:S(2)}) async-start(), calls=%async_computation.7 | async-start | bytes 1474560 | tf_op jit(solution)/shard_map/all_gather | solution.py:82
  90.0 158.0 %all-gather.18.cloned.1.call-start = ((), (), s32[]{:S(2)}) async-start(), calls=%async_computation.8 | async-start | bytes 2211840 | tf_op jit(solution)/shard_map/all_gather | solution.py:84
  90.6 221.5 %all-gather.20.cloned.1.call-start = ((), (), s32[]{:S(2)}) async-start(), calls=%async_computation.9 | async-start | bytes 4423680 | tf_op jit(solution)/shard_map/all_gather | solution.py:146
  91.2 247.7 %all-gather.22.cloned.1.call-start = ((), (), s32[]{:S(2)}) async-start(), calls=%async_computation.10 | async-start | bytes 1769472 | tf_op jit(solution)/shard_map/all_gather | solution.py:193
  91.2 21.6 %collective-permute-start = (bf16[192,2304]{1,0:T(8,128)(2,1)}, bf16[192,2304]{1,0:T(8,128)(2,1)S(1)}, u32[]{:S(2)}, u32[]{:S(2)}) collective-permute-start(bf16[192,2304]{1,0:T(8,128)(2,1)} %param.13), channel_id=1, source_target_pairs={{0,8},{8,0},{16,24},{24,16},{1,9},{9,1},{17,25},{25,17},{2,10},{10... | collective-permute-start | bytes 2654216 | tf_op jit(solution)/shard_map/ppermute | solution.py:71
  100.1 19.2 %copy-start.29 = (s32[1,1024]{1,0:T(1,128)}, s32[1,1024]{1,0:T(1,128)S(1)}, u32[]{:S(2)}) copy-start(s32[1,1024]{1,0:T(1,128)S(1)} %all-gather) | copy-start | bytes 12292
  100.2 43.1 %copy-start.12 = (pred[128,1024]{1,0:T(8,128)(4,1)}, pred[128,1024]{1,0:T(8,128)(4,1)S(1)}, u32[]{:S(2)}) copy-start(pred[128,1024]{1,0:T(8,128)(4,1)S(1)} %broadcast_compare_fusion.1) | copy-start | bytes 393220
  100.2 19.0 %copy-start.4 = (f32[128,12,64]{0,2,1:T(8,128)S(1)}, f32[128,12,64]{0,2,1:T(8,128)}, u32[]{:S(2)}) copy-start(f32[128,12,64]{0,2,1:T(8,128)} %copy-done.3) | copy-start | bytes 1179652
  100.2 19.0 %copy-start.19 = (f32[128,64]{0,1:T(8,128)S(1)}, f32[128,64]{0,1:T(8,128)}, u32[]{:S(2)}) copy-start(f32[128,64]{0,1:T(8,128)} %copy-done.18) | copy-start | bytes 98308
  116.2 126.3 %collective-permute-start.1 = (bf16[384,2304]{1,0:T(8,128)(2,1)}, bf16[384,2304]{1,0:T(8,128)(2,1)}, u32[]{:S(2)}, u32[]{:S(2)}) collective-permute-start(bf16[384,2304]{1,0:T(8,128)(2,1)} %maximum_select_fusion.2), channel_id=1, source_target_pairs={{0,16},{8,24},{16,0},{24,8},{1,17},{9,25},{17,1},{25,9},{2,18},{10... | collective-permute-start | bytes 5308424 | tf_op jit(solution)/shard_map/ppermute | solution.py:71
  117.3 250.8 %all-gather.24.cloned.1.call-start = ((), (), s32[]{:S(2)}) async-start(), calls=%async_computation.11 | async-start | bytes 1769472 | tf_op jit(solution)/shard_map/all_gather | solution.py:194
  120.6 2.7 copy-start
  125.2 23.9 %copy-start.31 = (f32[12,128]{1,0:T(8,128)}, f32[12,128]{1,0:T(8,128)S(1)}, u32[]{:S(2)}) copy-start(f32[12,128]{1,0:T(8,128)S(1)} %fusion.1) | copy-start | bytes 18436
  143.3 42.5 %copy-start.1 = (bf16[1,128,768]{2,1,0:T(8,128)(2,1)S(1)}, bf16[1,128,768]{2,1,0:T(8,128)(2,1)}, u32[]{:S(2)}) copy-start(bf16[1,128,768]{2,1,0:T(8,128)(2,1)} %param.9) | copy-start | bytes 589828
  149.1 38.6 %copy-start.17 = (bf16[128,12,64]{0,2,1:T(8,128)(2,1)}, bf16[128,12,64]{0,2,1:T(8,128)(2,1)S(1)}, u32[]{:S(2)}) copy-start(bf16[128,12,64]{0,2,1:T(8,128)(2,1)S(1)} %get-tuple-element.54) | copy-start | bytes 589828
  187.5 60.5 %copy-start.37 = (f32[128]{0:T(128)}, f32[128]{0:T(128)S(1)}, u32[]{:S(2)}) copy-start(f32[128]{0:T(128)S(1)} %broadcast_multiply_fusion.5) | copy-start | bytes 1540
  187.7 60.3 %copy-start.47 = (f32[128]{0:T(128)}, f32[128]{0:T(128)S(1)}, u32[]{:S(2)}) copy-start(f32[128]{0:T(128)S(1)} %multiply_reduce_fusion.3) | copy-start | bytes 1540
  187.8 60.2 %copy-start.40 = (f32[128]{0:T(128)}, f32[128]{0:T(128)S(1)}, u32[]{:S(2)}) copy-start(f32[128]{0:T(128)S(1)} %fusion.70) | copy-start | bytes 1540
  187.8 60.3 %copy-start.8 = (bf16[1,128,768]{2,1,0:T(8,128)(2,1)S(1)}, bf16[1,128,768]{2,1,0:T(8,128)(2,1)}, u32[]{:S(2)}) copy-start(bf16[1,128,768]{2,1,0:T(8,128)(2,1)} %param.17) | copy-start | bytes 589828
  248.1 3.8 copy-start.15
  251.9 64.4 %copy-start.14 = (bf16[128,1152]{1,0:T(8,128)(2,1)}, bf16[128,1152]{1,0:T(8,128)(2,1)S(1)}, u32[]{:S(2)}) copy-start(bf16[128,1152]{1,0:T(8,128)(2,1)S(1)} %get-tuple-element.24) | copy-start | bytes 884740
  252.7 63.6 %copy-start.5 = (bf16[128,1152]{1,0:T(8,128)(2,1)}, bf16[128,1152]{1,0:T(8,128)(2,1)S(1)}, u32[]{:S(2)}) copy-start(bf16[128,1152]{1,0:T(8,128)(2,1)S(1)} %get-tuple-element.26) | copy-start | bytes 884740
  312.1 4.1 copy-start.48
  312.1 4.2 copy-start.38
  312.1 4.2 copy-start.41
  312.1 4.9 copy-start.9
  312.1 5.0 copy-start.2
  316.6 0.5 copy-start.43
  318.5 80.5 %reduce-scatter.7.cloned.1.call-start = ((), (), s32[]{:S(2)}) async-start(), calls=%async_computation.13 | async-start | bytes 1474560 | tf_op jit(solution)/shard_map/reduce_scatter | solution.py:236
  320.9 117.2 %reduce-scatter.11.cloned.1.call-start = ((), (), s32[]{:S(2)}) async-start(), calls=%async_computation.15 | async-start | bytes 2211840 | tf_op jit(solution)/shard_map/reduce_scatter | solution.py:242
  323.9 6.3 copy-start.7
  323.9 182.2 %reduce-scatter.9.cloned.1.call-start = ((), (), s32[]{:S(2)}) async-start(), calls=%async_computation.14 | async-start | bytes 4423680 | tf_op jit(solution)/shard_map/reduce_scatter | solution.py:239
  328.0 0.7 copy-start.30
  328.0 247.0 %reduce-scatter.5.cloned.1.call-start = ((), (), s32[]{:S(2)}) async-start(), calls=%async_computation.12 | async-start | bytes 4423680 | tf_op jit(solution)/shard_map/reduce_scatter | solution.py:233
  342.2 10.3 %copy-start.32 = (f32[12,128]{1,0:T(8,128)}, f32[12,128]{1,0:T(8,128)S(1)}, u32[]{:S(2)}) copy-start(f32[12,128]{1,0:T(8,128)S(1)} %log_add_fusion) | copy-start | bytes 18436
  368.0 2.7 copy-start.23
  368.0 2.7 copy-start.24
  368.0 2.7 copy-start.26
  368.0 2.7 copy-start.28
  370.7 9.0 %copy-start.13 = (pred[128,1024]{1,0:T(8,128)(4,1)S(1)}, pred[128,1024]{1,0:T(8,128)(4,1)}, u32[]{:S(2)}) copy-start(pred[128,1024]{1,0:T(8,128)(4,1)} %copy-done.12) | copy-start | bytes 393220
  386.7 2.5 copy-start.11
  386.7 2.5 copy-start.25
  386.7 2.5 copy-start.27
  389.3 5.7 copy-start.34
  389.3 5.7 copy-start.36
  394.3 0.7 copy-start.21
  397.9 177.1 %copy-start.6 = (bf16[128,1152]{1,0:T(8,128)(2,1)S(1)}, bf16[128,1152]{1,0:T(8,128)(2,1)}, u32[]{:S(2)}) copy-start(bf16[128,1152]{1,0:T(8,128)(2,1)} %get-tuple-element.27) | copy-start | bytes 884740
  398.0 179.7 %copy-start.22 = (bf16[12,64,128]{2,1,0:T(8,128)(2,1)S(1)}, bf16[12,64,128]{2,1,0:T(8,128)(2,1)}, u32[]{:S(2)}) copy-start(bf16[12,64,128]{2,1,0:T(8,128)(2,1)} %copy-done.21) | copy-start | bytes 589828
  398.0 246.3 %all-reduce.10.cloned.1.call-start = ((), (), s32[]{:S(2)}) async-start(), calls=%async_computation.16 | async-start | bytes 5013504 | tf_op jit(solution)/shard_map/psum | solution.py:253
  577.7 3.4 copy-start.46
  577.7 3.7 copy-start.39
  577.7 27.7 %copy-start.10 = (bf16[1,128,768]{2,1,0:T(8,128)(2,1)S(1)}, bf16[1,128,768]{2,1,0:T(8,128)(2,1)}, u32[]{:S(2)}) copy-start(bf16[1,128,768]{2,1,0:T(8,128)(2,1)} %param.17) | copy-start | bytes 589828
  577.7 27.7 %copy-start.44 = (f32[128]{0:T(128)S(1)}, f32[128]{0:T(128)}, u32[]{:S(2)}) copy-start(f32[128]{0:T(128)} %copy-done.43) | copy-start | bytes 1540
  644.3 4.4 copy-start.16
  644.3 5.7 copy-start.20
Sparse Core Ops, SparseCore 0:
  9.6 72.7 all-gather.9
  88.8 24.2 all-gather.13
  115.0 25.7 all-gather.11
  142.2 43.5 all-gather.15
  187.2 54.5 all-gather.17
  243.2 68.8 all-gather.19
  314.6 24.2 all-gather.21
  340.8 25.8 all-gather.23
  369.1 29.1 reduce-scatter.6
  401.0 37.0 reduce-scatter.10
  440.6 65.4 reduce-scatter.8
  508.4 66.6 reduce-scatter.4
  579.2 65.0 all-reduce.9
